TPU v7x, 32 devices: a whole 2x2x4 slice. The times are simulated.
32 devices in a mesh: dp: 8 (over z, x), proto: 4 (over y, core).
Axes of the slice: x: 2, y: 2, z: 4, core: 2. Of those that a mesh axis runs over, the one named last changes fastest.
Arguments:
- teacher_feat: bfloat16 [4096, 256], P('dp'), may hold values from -16 to 16
- student_feat: bfloat16 [4096, 256], P('dp'), may hold values from -16 to 16
- teacher_protos: bfloat16 [65536, 256], P('proto'), may hold values from -16 to 16
- student_protos: bfloat16 [65536, 256], P('proto'), may hold values from -16 to 16
Outputs:
- row_loss: float32 [4096], P('dp')
- feature_grad: bfloat16 [4096, 256], P('dp')
- proto_grad: bfloat16 [65536, 256], P(('proto', 'dp'))
All inputs are finite; a program needn't handle non-finite values.
Results may differ from a plain program's by a relative error of at most 0.0069.
Values may be sent and summed in bfloat16 or wider, within the bound.
A program may use at most 192 MiB of HBM per device.

v0:
```python
import jax
import jax.numpy as jnp
from jax import lax
from jax.sharding import PartitionSpec as P

ITERS = 3


teacher_temp = 0.07
student_temp = 0.1


def unit_rows(x):
    xf = x.astype(jnp.float32)
    return (xf * lax.rsqrt(jnp.sum(xf * xf, axis=1, keepdims=True) + 1e-06)).astype(jnp.bfloat16)


def by_rows(left, right):
    return lax.dot_general(
        left, right, (((1,), (1,)), ((), ())), preferred_element_type=jnp.float32
    )


def by_cols(left, right):
    return lax.dot_general(
        left, right, (((0,), (0,)), ((), ())), preferred_element_type=jnp.float32
    )


def local(teacher_feat, student_feat, teacher_protos, student_protos):
    t_unit = unit_rows(teacher_feat)
    s_unit = unit_rows(student_feat)
    t_dirs = unit_rows(teacher_protos)
    s_dirs = unit_rows(student_protos)
    rows_local = t_unit.shape[0]
    protos_local = t_dirs.shape[0]
    data_count = lax.axis_size("dp")
    batch_total = rows_local * data_count
    proto_total = protos_local * lax.axis_size("proto")
    expo = jnp.exp(by_rows(t_unit, t_dirs) / teacher_temp)
    row_scale = jnp.ones((rows_local,), jnp.float32)
    col_scale = jnp.ones((protos_local,), jnp.float32)
    row_total = jnp.ones((rows_local,), jnp.float32)
    for step in range(ITERS):
        local_col = jnp.dot(
            row_scale, expo, precision=lax.Precision.HIGHEST, preferred_element_type=jnp.float32
        )
        col_whole = lax.psum(local_col, "dp")
        col_scale = 1.0 / (proto_total * col_whole)
        local_row = jnp.dot(
            expo, col_scale, precision=lax.Precision.HIGHEST, preferred_element_type=jnp.float32
        )
        row_total = lax.psum(local_row, "proto")
        row_scale = 1.0 / (batch_total * row_total)
    targets = expo * col_scale[None, :] / row_total[:, None]
    logits = by_rows(s_unit, s_dirs) / student_temp
    expl = jnp.exp(logits)
    totals, cross = lax.psum((jnp.sum(expl, axis=1), jnp.sum(targets * logits, axis=1)), "proto")
    row_loss = jnp.log(totals) - cross
    factor = proto_total / (batch_total * student_temp)
    dlog = ((expl / totals[:, None] - targets) * factor).astype(jnp.bfloat16)
    feature_terms = jnp.dot(dlog, s_dirs, preferred_element_type=jnp.float32)
    feature_grad = lax.psum(feature_terms, "proto").astype(jnp.bfloat16)
    proto_grad = lax.psum_scatter(by_cols(dlog, s_unit), "dp", scatter_dimension=0, tiled=True)
    return (row_loss, feature_grad, proto_grad.astype(jnp.bfloat16))


def solution(mesh):
    placed = (P("dp", None), P("dp", None), P("proto", None), P("proto", None))
    return jax.shard_map(
        local,
        mesh=mesh,
        in_specs=placed,
        out_specs=(P("dp"), P("dp", None), P(("proto", "dp"), None)),
        check_vma=False,
    )
```

profile of v0, /device:TPU:0, one launch (start us, length us, event | category | flops | bytes accessed | tf_op | source)
XLA Modules:
  0.0 789.9 jit_solution(12810597469447862436)
XLA Ops:
  7.2 0.0 all-reduce.6.cloned.1.call-start
  7.2 1.1 fusion.12
  8.3 5.2 fusion.2
  13.6 16.0 %multiply_exponential_fusion = f32[512,16384]{1,0:T(8,128)} fusion(bf16[16384,256]{1,0:T(8,128)(2,1)} %param.6, f32[16384]{0:T(1024)S(1)} %add_rsqrt_fusion, bf16[512,256]{1,0:T(8,128)(2,1)} %param.4, f32[512]{0:T(512)S(1)} %add_rsqrt_fusion.2), kind=kOutput, calls=%fused_computation.3 | convolution fusion | flops 4316332032 | bytes 42272768 | tf_op jit(solution)/shard_map/dot_general | solution.py:19
  29.5 20.1 %fusion.19 = f32[1,16384]{1,0:T(1,128)} fusion(f32[512,16384]{1,0:T(8,128)} %multiply_exponential_fusion), kind=kOutput, calls=%fused_computation.36 | convolution fusion | flops 100663296 | bytes 33619968 | tf_op jit(solution)/shard_map/dot_general | solution.py:45
  49.7 0.0 all-reduce.6.cloned.1.call-update
  49.7 0.5 all-reduce.8.cloned.1.call-start
  50.2 5.2 fusion
  55.5 65.6 %all-reduce.6.cloned.1.call-done = f32[16384]{0:T(1024)} async-done(((f32[16384]{0:T(1024)}), f32[16384]{0:T(1024)}) %all-reduce.6.cloned.1.call-update) | async-done | bytes 65552 | tf_op jit(solution)/shard_map/psum | solution.py:48
  121.0 0.9 multiply_divide_fusion.3
  121.9 0.0 copy-start
  121.9 31.9 %fusion.22 = f32[1,512]{1,0:T(1,128)S(1)} fusion(f32[512,16384]{1,0:T(8,128)} %multiply_exponential_fusion, f32[16384,1]{0,1:T(1,128)S(1)} %bitcast.28), kind=kOutput, calls=%fused_computation.39 | convolution fusion | flops 100663296 | bytes 33622016 | tf_op jit(solution)/shard_map/dot_general | solution.py:50
  153.8 5.7 psum.65
  159.5 20.1 %fusion.23 = f32[1,16384]{1,0:T(1,128)} fusion(f32[512,1]{0,1:T(1,128)S(1)} %bitcast.31, f32[512,16384]{1,0:T(8,128)} %multiply_exponential_fusion), kind=kOutput, calls=%fused_computation.40 | convolution fusion | flops 100663296 | bytes 33622016 | tf_op jit(solution)/shard_map/dot_general | solution.py:45
  179.6 0.0 all-reduce.8.cloned.1.call-update
  179.7 0.2 all-reduce.10.cloned.1.call-start
  179.9 0.0 copy-done
  179.9 0.1 fusion.10
  180.0 68.4 %all-reduce.8.cloned.1.call-done = f32[16384]{0:T(1024)} async-done(((f32[16384]{0:T(1024)}), f32[16384]{0:T(1024)}) %all-reduce.8.cloned.1.call-update) | async-done | bytes 65552 | tf_op jit(solution)/shard_map/psum | solution.py:48
  248.5 0.9 multiply_divide_fusion.2
  249.3 31.9 %fusion.24 = f32[1,512]{1,0:T(1,128)S(1)} fusion(f32[512,16384]{1,0:T(8,128)} %multiply_exponential_fusion, f32[16384,1]{0,1:T(1,128)S(1)} %bitcast.29), kind=kOutput, calls=%fused_computation.41 | convolution fusion | flops 100663296 | bytes 33622016 | tf_op jit(solution)/shard_map/dot_general | solution.py:50
  281.2 5.7 psum.67
  286.9 20.1 %fusion.25 = f32[1,16384]{1,0:T(1,128)} fusion(f32[512,1]{0,1:T(1,128)S(1)} %bitcast.33, f32[512,16384]{1,0:T(8,128)} %multiply_exponential_fusion), kind=kOutput, calls=%fused_computation.42 | convolution fusion | flops 100663296 | bytes 33622016 | tf_op jit(solution)/shard_map/dot_general | solution.py:45
  307.0 0.0 all-reduce.10.cloned.1.call-update
  307.0 0.3 reduce-scatter.2.cloned.1.call-start
  307.3 68.5 %all-reduce.10.cloned.1.call-done = f32[16384]{0:T(1024)} async-done(((f32[16384]{0:T(1024)}), f32[16384]{0:T(1024)}) %all-reduce.10.cloned.1.call-update) | async-done | bytes 65552 | tf_op jit(solution)/shard_map/psum | solution.py:48
  375.8 0.9 multiply_divide_fusion.1
  376.7 31.9 %fusion.26 = f32[1,512]{1,0:T(1,128)S(1)} fusion(f32[512,16384]{1,0:T(8,128)} %multiply_exponential_fusion, f32[16384,1]{0,1:T(1,128)S(1)} %bitcast.24), kind=kOutput, calls=%fused_computation.43 | convolution fusion | flops 100663296 | bytes 33622016 | tf_op jit(solution)/shard_map/dot_general | solution.py:50
  408.5 5.7 psum.69
  414.2 33.8 %exponential_reduce_fusion = (f32[512]{0:T(512)S(1)}, f32[512]{0:T(512)S(1)}, f32[512,16384]{1,0:T(8,128)}) fusion(f32[512]{0:T(512)S(1)} %psum.69, f32[512,16384]{1,0:T(8,128)} %multiply_exponential_fusion, f32[16384]{0:T(1024)S(1)} %multiply_divide_fusion.1, bf16[16384,256]{1,0:T(8,128)(2,1)} %param.7, f32[16384]{0:T(1024)S(1)} %add_rsqrt_fusion.1, ...), kind=kOutput, calls=%fused_computation.4 | convolution fusion | flops 4358274048 | bytes 75898880 | tf_op jit(solution)/shard_map/dot_general | solution.py:19
  448.0 6.8 psum.63
  454.9 27.7 %multiply_convert_fusion = bf16[512,16384]{1,0:T(8,128)(2,1)} fusion(f32[512,16384]{1,0:T(8,128)} %get-tuple-element.7, f32[512]{0:T(512)S(1)} %psum.63, f32[512]{0:T(512)S(1)} %psum.69, f32[512,16384]{1,0:T(8,128)} %multiply_exponential_fusion, f32[16384]{0:T(1024)S(1)} %multiply_divide_fusion.1), kind=kLoop, calls=%fused_computation | loop fusion | flops 58720256 | bytes 83955712 | tf_op jit(solution)/shard_map/convert_element_type | solution.py:61
  482.5 16.2 %fusion.16 = f32[16384,256]{1,0:T(8,128)} fusion(bf16[512,16384]{1,0:T(8,128)(2,1)} %multiply_convert_fusion, bf16[512,256]{1,0:T(8,128)(2,1)S(1)} %copy-done, f32[512]{0:T(512)S(1)} %add_rsqrt_fusion.3), kind=kOutput, calls=%fused_computation.25 | convolution fusion | flops 4295360512 | bytes 33818624 | tf_op jit(solution)/shard_map/dot_general | solution.py:25
  498.7 0.0 reduce-scatter.2.cloned.1.call-update
  498.7 12.6 %fusion.6 = f32[512,256]{1,0:T(8,128)S(1)} fusion(bf16[512,16384]{1,0:T(8,128)(2,1)} %multiply_convert_fusion, bf16[16384,256]{1,0:T(8,128)(2,1)} %param.7, f32[16384]{0:T(1024)S(1)} %add_rsqrt_fusion.1), kind=kOutput, calls=%fused_computation.14 | convolution fusion | flops 4307550208 | bytes 25755648 | tf_op jit(solution)/shard_map/dot_general | solution.py:62
  511.3 17.7 %all-reduce.11 = (f32[512]{0:T(512)S(1)}, bf16[512,256]{1,0:T(8,128)(2,1)}) all-reduce(f32[512]{0:T(512)S(1)} %get-tuple-element.4, f32[512,256]{1,0:T(8,128)S(1)} %fusion.6), channel_id=1, replica_groups=mesh['dp'=8,'proto'=4] {'proto'}, use_global_device_ids=true, to_apply=%region_13.0 | all-reduce | flops 131584 | bytes 790528 | tf_op jit(solution)/shard_map/psum | solution.py:58
  529.0 0.6 log_subtract_fusion
  529.6 250.6 %reduce-scatter.2.cloned.1.call-done = f32[2048,256]{1,0:T(8,128)} async-done(((f32[16384,256]{1,0:T(8,128)}), f32[2048,256]{1,0:T(8,128)}) %reduce-scatter.2.cloned.1.call-update) | async-done | bytes 2097168 | tf_op jit(solution)/shard_map/reduce_scatter | solution.py:64
  780.2 2.7 convert_element_type.43
  (6 shorter events, 0.1 us)
Async XLA Ops:
  7.2 113.9 %all-reduce.6.cloned.1.call-start = ((), (), s32[]{:S(2)}) async-start(), calls=%async_computation.1 | async-start | bytes 131072 | tf_op jit(solution)/shard_map/psum | solution.py:48
  49.7 198.8 %all-reduce.8.cloned.1.call-start = ((), (), s32[]{:S(2)}) async-start(), calls=%async_computation.2 | async-start | bytes 131072 | tf_op jit(solution)/shard_map/psum | solution.py:48
  121.9 58.0 %copy-start = (bf16[512,256]{1,0:T(8,128)(2,1)S(1)}, bf16[512,256]{1,0:T(8,128)(2,1)}, u32[]{:S(2)}) copy-start(bf16[512,256]{1,0:T(8,128)(2,1)} %param.5) | copy-start | bytes 786436
  179.7 196.2 %all-reduce.10.cloned.1.call-start = ((), (), s32[]{:S(2)}) async-start(), calls=%async_computation.3 | async-start | bytes 131072 | tf_op jit(solution)/shard_map/psum | solution.py:48
  307.0 473.2 %reduce-scatter.2.cloned.1.call-start = ((), (), s32[]{:S(2)}) async-start(), calls=%async_computation.4 | async-start | bytes 18874368 | tf_op jit(solution)/shard_map/reduce_scatter | solution.py:64
Sparse Core Ops, SparseCore 0:
  49.8 71.1 all-reduce.5
  179.8 68.6 all-reduce.7
  307.1 68.6 all-reduce.9
  498.8 281.3 reduce-scatter.1
where the time goes:
time: 796 us; the launch traced here: 790 us
  waiting for transfers between devices  453 us (57%)
  matrix products  235 us (30%)
  other arithmetic  45.2 us (6%)
  blocking collectives  41.5 us (5%)
  between operations  14.3 us (2%)
    reduce_scatter x1, waiting for transfers between devices, local(): lax.psum_scatter(by_cols(dlog, s_unit), 'dp', scatter_dimension=0, tiled=...  251 us
    psum x3, waiting for transfers between devices, local(): col_whole = lax.psum(local_col, 'dp')  203 us
    dot_general x3, matrix products, local(): jnp.dot(expo, col_scale, precision=lax.Precision.HIGHEST, preferred_eleme...  95.6 us
    dot_general x3, matrix products, local(): jnp.dot(row_scale, expo, precision=lax.Precision.HIGHEST, preferred_eleme...  60.4 us
    dot_general x2, matrix products, by_rows(): lax.dot_general(left, right, (((1,), (1,)), ((), ())), preferred_element_...  49.8 us
    convert_element_type x1, other arithmetic, local(): dlog = ((expl / totals[:, None] - targets) * factor).astype(jnp.bfloat16)  27.7 us
    psum x2, blocking collectives, local(): lax.psum((jnp.sum(expl, axis=1), jnp.sum(targets * logits, axis=1)), 'pro...  24.5 us
    psum x3, blocking collectives, local(): row_total = lax.psum(local_row, 'proto')  17 us
  transfers between devices with their start and end apart: 4, of which 4 were waited for; matrix products, arithmetic and copies ran while one was open for 2% of the time, Pallas kernels for 0%

commit v1 on v0

v1 whole, which is shorter than its diff:
```python
import jax
import jax.numpy as jnp
from jax import lax
from jax.sharding import PartitionSpec as P

ITERS = 3


teacher_temp = 0.07
student_temp = 0.1


def unit_rows(x):
    xf = x.astype(jnp.float32)
    return (xf * lax.rsqrt(jnp.sum(xf * xf, axis=1, keepdims=True) + 1e-06)).astype(jnp.bfloat16)


def by_rows(left, right):
    return lax.dot_general(
        left, right, (((1,), (1,)), ((), ())), preferred_element_type=jnp.float32
    )


def by_cols(left, right):
    return lax.dot_general(
        left, right, (((0,), (0,)), ((), ())), preferred_element_type=jnp.float32
    )


def local(teacher_feat, student_feat, teacher_protos, student_protos):
    both = ("dp", "proto")
    data_count = lax.axis_size("dp")
    mine = teacher_protos.shape[0] // data_count
    start = lax.axis_index("dp") * mine
    t_unit = lax.all_gather(unit_rows(teacher_feat), "dp", tiled=True)
    s_unit = lax.all_gather(unit_rows(student_feat), "dp", tiled=True)
    t_dirs = unit_rows(lax.dynamic_slice_in_dim(teacher_protos, start, mine, 0))
    s_dirs = unit_rows(lax.dynamic_slice_in_dim(student_protos, start, mine, 0))
    batch_total = t_unit.shape[0]
    proto_total = mine * data_count * lax.axis_size("proto")
    expo = jnp.exp(by_rows(t_unit, t_dirs) / teacher_temp)
    row_scale = jnp.ones((batch_total,), jnp.float32)
    for step in range(ITERS):
        col_scale = 1.0 / (proto_total * jnp.sum(expo * row_scale[:, None], axis=0))
        row_total = lax.psum(jnp.sum(expo * col_scale[None, :], axis=1), both)
        row_scale = 1.0 / (batch_total * row_total)
    targets = expo * col_scale[None, :] / row_total[:, None]
    logits = by_rows(s_unit, s_dirs) / student_temp
    expl = jnp.exp(logits)
    totals, cross = lax.psum((jnp.sum(expl, axis=1), jnp.sum(targets * logits, axis=1)), both)
    row_loss = jnp.log(totals) - cross
    rows_local = teacher_feat.shape[0]
    row_loss = lax.dynamic_slice_in_dim(row_loss, lax.axis_index("dp") * rows_local, rows_local, 0)
    factor = proto_total / (batch_total * student_temp)
    dlog = ((expl / totals[:, None] - targets) * factor).astype(jnp.bfloat16)
    proto_grad = by_cols(dlog, s_unit).astype(jnp.bfloat16)
    feature_terms = jnp.dot(dlog, s_dirs, preferred_element_type=jnp.float32)
    feature_grad = lax.psum_scatter(feature_terms, "dp", scatter_dimension=0, tiled=True)
    feature_grad = lax.psum(feature_grad, "proto").astype(jnp.bfloat16)
    return (row_loss, feature_grad, proto_grad)


def solution(mesh):
    placed = (P("dp", None), P("dp", None), P("proto", None), P("proto", None))
    return jax.shard_map(
        local,
        mesh=mesh,
        in_specs=placed,
        out_specs=(P("dp"), P("dp", None), P(("proto", "dp"), None)),
        check_vma=False,
    )
```

time: 796 us -> 484 us (0.61)
  waiting for transfers between devices: 453 us -> 124 us
  matrix products: 235 us -> 66.2 us
  blocking collectives: 41.5 us -> 179 us
  other arithmetic: 45.2 us -> 100 us
    psum x3 -> x0, waiting for transfers between devices: 203 us -> none  [local(): col_whole = lax.psum(local_col, 'dp')]
    reduce_scatter x1, waiting for transfers between devices: 251 us -> 77.9 us  [local(): lax.psum_scatter(feature_terms, 'dp', scatter_dimension=0, tiled=True)]
    dot_general x6 -> x0, matrix products: 156 us -> none  [the longest x3 95.6 us: local(): jnp.dot(expo, col_scale, precision=lax.Precision.HIGHEST, preferred_eleme...]
    psum x5, blocking collectives: 41.5 us -> 179 us  [the longest x3 121 us: local(): row_total = lax.psum(jnp.sum(expo * col_scale[None, :], axis=1), both)]
    reduce_sum x0 -> x5, other arithmetic: none -> 62.9 us  [the longest x3 38.4 us: local(): row_total = lax.psum(jnp.sum(expo * col_scale[None, :], axis=1), both)]
    all_gather x0 -> x2, waiting for transfers between devices: none -> 46.4 us  [the longest x1 46.4 us: local(): t_unit = lax.all_gather(unit_rows(teacher_feat), 'dp', tiled=True)]
  transfers between devices with their start and end apart: 4 -> 3, of which waited for: 4 -> 2; matrix products, arithmetic and copies ran while one was open for 2% -> 20% of each run, Pallas kernels for 0% -> 0%
where the time goes in v1:
time: 484 us; the launch traced here: 483 us
  blocking collectives  179 us (37%)
  waiting for transfers between devices  124 us (26%)
  other arithmetic  100 us (21%)
  matrix products  66.2 us (14%)
  between operations  13.9 us (3%)
    psum x3, blocking collectives, local(): row_total = lax.psum(jnp.sum(expo * col_scale[None, :], axis=1), both)  121 us
    reduce_scatter x1, waiting for transfers between devices, local(): lax.psum_scatter(feature_terms, 'dp', scatter_dimension=0, tiled=True)  77.9 us
    all_gather x1, waiting for transfers between devices, local(): t_unit = lax.all_gather(unit_rows(teacher_feat), 'dp', tiled=True)  46.4 us
    dot_general x2, matrix products, by_rows(): lax.dot_general(left, right, (((1,), (1,)), ((), ())), preferred_element_...  43.8 us
    psum x1, blocking collectives, local(): lax.psum((jnp.sum(expl, axis=1), jnp.sum(targets * logits, axis=1)), both)  39.5 us
    reduce_sum x3, other arithmetic, local(): row_total = lax.psum(jnp.sum(expo * col_scale[None, :], axis=1), both)  38.4 us
    convert_element_type x1, other arithmetic, local(): dlog = ((expl / totals[:, None] - targets) * factor).astype(jnp.bfloat16)  27.6 us
    reduce_sum x2, other arithmetic, local(): col_scale = 1.0 / (proto_total * jnp.sum(expo * row_scale[:, None], axis=0))  24.5 us
  transfers between devices with their start and end apart: 3, of which 2 were waited for; matrix products, arithmetic and copies ran while one was open for 20% of the time, Pallas kernels for 0%

profile of v1, /device:TPU:0, one launch (start us, length us, event | category | flops | bytes accessed | tf_op | source)
XLA Modules:
  0.0 483.3 jit_solution(18347640859334793745)
XLA Ops:
  7.2 0.0 all-gather.5.cloned.1.call-start
  7.2 1.1 fusion.9
  8.3 1.8 fusion.10
  10.1 0.0 all-gather.5.cloned.1.call-update
  10.1 0.0 all-gather.3.cloned.1.call-start
  10.2 1.1 fusion.7
  11.3 1.8 fusion.8
  13.1 0.0 all-gather.3.cloned.1.call-update
  13.1 0.0 reduce-scatter.2.cloned.1.call-start
  13.2 1.6 fusion.2
  14.8 1.6 fusion
  16.4 46.4 %all-gather.5.cloned.1.call-done = bf16[4096,256]{1,0:T(8,128)(2,1)} async-done(((bf16[512,256]{1,0:T(8,128)(2,1)}), bf16[4096,256]{1,0:T(8,128)(2,1)}) %all-gather.5.cloned.1.call-update) | async-done | bytes 2097168 | tf_op jit(solution)/shard_map/all_gather | solution.py:35
  62.7 15.5 %fusion.18 = (f32[2048]{0:T(1024)S(1)}, f32[4096,2048]{0,1:T(8,128)}) fusion(bf16[4096,256]{1,0:T(8,128)(2,1)} %all-gather.5.cloned.1.call-done, f32[2048]{0:T(1024)S(1)} %add_rsqrt_fusion, bf16[16384,256]{1,0:T(8,128)(2,1)} %param.6, s32[]{:T(128)S(6)} %select_n.7), kind=kOutput, calls=%fused_computation.45 | convolution fusion | flops 4313315328 | bytes 36716548 | tf_op jit(solution)/shard_map/dot_general | solution.py:19
  78.3 12.8 %multiply_reduce_fusion.4 = f32[4096]{0:T(1024)S(1)} fusion(f32[4096,2048]{0,1:T(8,128)} %get-tuple-element.8, f32[2048]{0:T(1024)S(1)} %multiply_divide_fusion.5), kind=kLoop, calls=%fused_computation.5 | loop fusion | flops 16773120 | bytes 33579008 | tf_op jit(solution)/shard_map/reduce_sum | solution.py:45
  91.1 40.6 %psum.43 = f32[4096]{0:T(1024)S(1)} all-reduce(f32[4096]{0:T(1024)S(1)} %multiply_reduce_fusion.4), channel_id=1, replica_groups=mesh['dp'=8,'proto'=4] {'dp','proto'}, use_global_device_ids=true, to_apply=%region_8.0 | all-reduce | flops 4096 | bytes 32768 | tf_op jit(solution)/shard_map/psum | solution.py:45
  131.7 12.3 %multiply_reduce_fusion.3 = f32[2048]{0:T(1024)S(1)} fusion(f32[4096,2048]{0,1:T(8,128)} %get-tuple-element.8, f32[4096]{0:T(1024)S(1)} %multiply_divide_fusion.2), kind=kLoop, calls=%fused_computation.4 | loop fusion | flops 16775168 | bytes 33579008 | tf_op jit(solution)/shard_map/reduce_sum | solution.py:44
  143.9 12.8 %multiply_reduce_fusion.2 = f32[4096]{0:T(1024)S(1)} fusion(f32[4096,2048]{0,1:T(8,128)} %get-tuple-element.8, f32[2048]{0:T(1024)S(1)} %multiply_divide_fusion.4), kind=kLoop, calls=%fused_computation.3 | loop fusion | flops 16773120 | bytes 33579008 | tf_op jit(solution)/shard_map/reduce_sum | solution.py:45
  156.7 39.4 %psum.44 = f32[4096]{0:T(1024)S(1)} all-reduce(f32[4096]{0:T(1024)S(1)} %multiply_reduce_fusion.2), channel_id=1, replica_groups=mesh['dp'=8,'proto'=4] {'dp','proto'}, use_global_device_ids=true, to_apply=%region_11.0 | all-reduce | flops 4096 | bytes 32768 | tf_op jit(solution)/shard_map/psum | solution.py:45
  196.2 12.3 %multiply_reduce_fusion.1 = f32[2048]{0:T(1024)S(1)} fusion(f32[4096,2048]{0,1:T(8,128)} %get-tuple-element.8, f32[4096]{0:T(1024)S(1)} %multiply_divide_fusion.1), kind=kLoop, calls=%fused_computation.2 | loop fusion | flops 16775168 | bytes 33579008 | tf_op jit(solution)/shard_map/reduce_sum | solution.py:44
  208.4 12.8 %multiply_reduce_fusion.5 = f32[4096]{0:T(1024)S(1)} fusion(f32[4096,2048]{0,1:T(8,128)} %get-tuple-element.8, f32[2048]{0:T(1024)S(1)} %multiply_divide_fusion.3), kind=kLoop, calls=%fused_computation.8 | loop fusion | flops 16773120 | bytes 33579008 | tf_op jit(solution)/shard_map/reduce_sum | solution.py:45
  221.2 41.0 %psum.45 = f32[4096]{0:T(1024)S(1)} all-reduce(f32[4096]{0:T(1024)S(1)} %multiply_reduce_fusion.5), channel_id=1, replica_groups=mesh['dp'=8,'proto'=4] {'dp','proto'}, use_global_device_ids=true, to_apply=%region_14.0 | all-reduce | flops 4096 | bytes 32768 | tf_op jit(solution)/shard_map/psum | solution.py:45
  262.3 0.0 all-gather.3.cloned.1.call-done
  262.3 28.3 %exponential_reduce_fusion = (f32[4096]{0:T(1024)S(1)}, f32[4096]{0:T(1024)S(1)}, f32[4096,2048]{0,1:T(8,128)}) fusion(f32[4096]{0:T(1024)S(1)} %psum.45, f32[4096,2048]{0,1:T(8,128)} %get-tuple-element.8, f32[2048]{0:T(1024)S(1)} %multiply_divide_fusion.3, bf16[4096,256]{1,0:T(8,128)(2,1)} %all-gather.3.cloned.1.call-done, f32[2048]{0:T(1024)S(1)} %add_rsqrt_fusion.1, ...), kind=kOutput, calls=%fused_computation.9 | convolution fusion | flops 4346863616 | bytes 70320128 | tf_op jit(solution)/shard_map/dot_general | solution.py:19
  290.6 39.5 %all-reduce = (f32[4096]{0:T(1024)S(1)}, f32[4096]{0:T(1024)S(1)}) all-reduce(f32[4096]{0:T(1024)S(1)} %get-tuple-element.4, f32[4096]{0:T(1024)S(1)} %get-tuple-element.3), channel_id=1, replica_groups=mesh['dp'=8,'proto'=4] {'dp','proto'}, use_global_device_ids=true, to_apply=%region_16.0 | all-reduce | flops 8192 | bytes 65536 | tf_op jit(solution)/shard_map/psum | solution.py:50
  330.1 27.6 %multiply_convert_fusion = bf16[4096,2048]{0,1:T(8,128)(2,1)} fusion(f32[4096,2048]{0,1:T(8,128)} %get-tuple-element.9, f32[4096]{0:T(1024)S(1)} %get-tuple-element.6, f32[4096]{0:T(1024)S(1)} %psum.45, f32[4096,2048]{0,1:T(8,128)} %get-tuple-element.8, f32[2048]{0:T(1024)S(1)} %multiply_divide_fusion.3), kind=kLoop, calls=%fused_computation | loop fusion | flops 58720256 | bytes 83927040 | tf_op jit(solution)/shard_map/convert_element_type | solution.py:55
  357.7 0.0 copy-start
  357.7 13.2 %fusion.11 = f32[4096,256]{1,0:T(8,128)} fusion(bf16[4096,2048]{0,1:T(8,128)(2,1)} %multiply_convert_fusion, f32[2048]{0:T(1024)S(1)} %add_rsqrt_fusion.1, bf16[16384,256]{1,0:T(8,128)(2,1)} %param.7, s32[]{:T(128)S(6)} %select_n.7), kind=kOutput, calls=%fused_computation.29 | convolution fusion | flops 4296540160 | bytes 22028292 | tf_op jit(solution)/shard_map/dot_general | solution.py:57
  370.8 0.0 reduce-scatter.2.cloned.1.call-update
  370.9 0.7 dynamic-slice_subtract_fusion
  371.5 0.0 copy-done
  371.5 9.2 %convolution_convert_fusion = bf16[2048,256]{1,0:T(8,128)(2,1)} fusion(bf16[4096,2048]{0,1:T(8,128)(2,1)} %multiply_convert_fusion, bf16[4096,256]{1,0:T(8,128)(2,1)S(1)} %copy-done), kind=kOutput, calls=%fused_computation.14 | convolution fusion | flops 4295491584 | bytes 19922944 | tf_op jit(solution)/shard_map/dot_general | solution.py:25
  380.7 77.9 %reduce-scatter.2.cloned.1.call-done = f32[512,256]{1,0:T(8,128)} async-done(((f32[4096,256]{1,0:T(8,128)}), f32[512,256]{1,0:T(8,128)}) %reduce-scatter.2.cloned.1.call-update) | async-done | bytes 524304 | tf_op jit(solution)/shard_map/reduce_scatter | solution.py:58
  458.7 18.1 %all-reduce.2 = bf16[512,256]{1,0:T(8,128)(2,1)} all-reduce(f32[512,256]{1,0:T(8,128)} %reduce-scatter.2.cloned.1.call-done), channel_id=1, replica_groups=mesh['dp'=8,'proto'=4] {'proto'}, use_global_device_ids=true, to_apply=%region_18.0 | all-reduce | flops 131072 | bytes 786432 | tf_op jit(solution)/shard_map/psum | solution.py:59
  (9 shorter events, 0.1 us)
Async XLA Ops:
  7.2 55.6 %all-gather.5.cloned.1.call-start = ((), (), s32[]{:S(2)}) async-start(), calls=%async_computation.2 | async-start | bytes 2359296 | tf_op jit(solution)/shard_map/all_gather | solution.py:35
  10.1 252.1 %all-gather.3.cloned.1.call-start = ((), (), s32[]{:S(2)}) async-start(), calls=%async_computation.1 | async-start | bytes 2359296 | tf_op jit(solution)/shard_map/all_gather | solution.py:36
  13.1 445.5 %reduce-scatter.2.cloned.1.call-start = ((), (), s32[]{:S(2)}) async-start(), calls=%async_computation.3 | async-start | bytes 4718592 | tf_op jit(solution)/shard_map/reduce_scatter | solution.py:58
  357.7 13.9 %copy-start = (bf16[4096,256]{1,0:T(8,128)(2,1)S(1)}, bf16[4096,256]{1,0:T(8,128)(2,1)}, u32[]{:S(2)}) copy-start(bf16[4096,256]{1,0:T(8,128)(2,1)} %all-gather.3.cloned.1.call-done) | copy-start | bytes 6291460
Sparse Core Ops, SparseCore 0:
  10.7 51.9 all-gather.4
  65.4 48.8 all-gather.2
  371.0 87.6 reduce-scatter.1

commit v2 on v1

v2 whole, which is shorter than its diff:
```python
import functools
import math

import jax
import jax.numpy as jnp
from jax import lax
from jax.experimental import pallas as pl
from jax.experimental.pallas import tpu as pltpu
from jax.sharding import PartitionSpec as P

ITERS = 3
teacher_temp = 0.07
student_temp = 0.1
LOG2E = math.log2(math.e)
MESH = pl.DeviceIdType.MESH
f32, bf16 = jnp.float32, jnp.bfloat16


def unit_rows(x):
    xf = x.astype(f32)
    return (xf * lax.rsqrt(jnp.sum(xf * xf, axis=1, keepdims=True) + 1e-06)).astype(bf16)


def by_rows(left, right):
    return lax.dot_general(left, right, (((1,), (1,)), ((), ())), preferred_element_type=f32)


def by_cols(left, right):
    return lax.dot_general(left, right, (((0,), (0,)), ((), ())), preferred_element_type=f32)


def split16(x):
    n = x.shape[1]
    hi = x.astype(bf16).astype(f32)
    row = lax.broadcasted_iota(jnp.int32, (16, n), 0)
    return jnp.where(row == 0, hi, jnp.where(row == 1, x - hi, 0.0)).astype(bf16)


def kernel(
    D, Q, tf, sf, tp, sp, stats, fterm, pg,
    tdir, sdir, tu, su, expo, expl, dblk, acc, colv, vec, rowp, part, b1, b2, fin,
    load_sem, gs, gr, asem, rsem,
):
    R, K = tf.shape
    M = tdir.shape[0]
    B = D * R
    NZ, PS = D // 2, 2 * Q
    C = B // PS
    per = C // R
    H = R // 2
    NC = min(M, 512)
    protos = M * D * Q
    dp, q = lax.axis_index("dp"), lax.axis_index("proto")
    z, x, c = dp // 2, lax.rem(dp, 2), lax.rem(q, 2)
    p = q + Q * x
    core = q + 1 - 2 * c

    def plane(j):
        p2 = lax.rem(p + j, PS)
        return p2, {"dp": z * 2 + p2 // Q, "proto": lax.rem(p2, Q)}

    def column(j):
        return {"dp": lax.rem(z + j, NZ) * 2 + x, "proto": q}

    loads = [
        pltpu.make_async_copy(src.at[pl.ds(pl.multiple_of(dp * M, M), M), :], dst, load_sem.at[n])
        for n, (src, dst) in enumerate(((tp, tdir), (sp, sdir)))
    ]
    for cp in loads:
        cp.start()

    barrier = pltpu.get_barrier_semaphore()
    for j in range(1, PS):
        pl.semaphore_signal(barrier, inc=1, device_id=plane(j)[1], device_id_type=MESH)
    for j in range(1, NZ):
        pl.semaphore_signal(barrier, inc=1, device_id=column(j), device_id_type=MESH)

    tu[pl.ds(pl.multiple_of(dp * R, R), R), :] = unit_rows(tf[...])
    su[pl.ds(pl.multiple_of(dp * R, R), R), :] = unit_rows(sf[...])
    pl.semaphore_wait(barrier, PS - 1 + NZ - 1)

    bufs = (tu, su)
    RIGHT, LEFT, ACROSS, OTHER = range(4)

    def half(t, d, cc):
        return bufs[t].at[pl.ds(pl.multiple_of(d * R + cc * H, H), H), :]

    def move(t, route, d):
        dev = (
            {"dp": lax.min(dp + 2, D - 2 + x), "proto": q},
            {"dp": lax.max(dp - 2, x), "proto": q},
            {"dp": z * 2 + 1 - x, "proto": q},
            {"dp": dp, "proto": core},
        )[route]
        return pltpu.make_async_remote_copy(
            src_ref=half(t, d, c), dst_ref=half(t, d, c),
            send_sem=gs.at[t, route, d], recv_sem=gr.at[t, d, c],
            device_id=dev, device_id_type=MESH,
        )

    def arrived(t, d, cc):
        pltpu.make_async_remote_copy(
            src_ref=half(t, d, cc), dst_ref=half(t, d, cc),
            send_sem=gs.at[t, 0, d], recv_sem=gr.at[t, d, cc],
            device_id={"dp": dp, "proto": core}, device_id_type=MESH,
        ).wait_recv()

    def go(t, route, d):
        move(t, route, d).start()

    def start_own(t):
        pl.when(z < NZ - 1)(lambda: go(t, RIGHT, dp))
        pl.when(z > 0)(lambda: go(t, LEFT, dp))
        go(t, ACROSS, dp)

    def along(t, s):
        @pl.when(z - s >= 0)
        def _():
            d = (z - s) * 2 + x
            arrived(t, d, c)
            pl.when(z < NZ - 1)(lambda: go(t, RIGHT, d))
            go(t, ACROSS, d)
            go(t, OTHER, d)

        @pl.when(z + s < NZ)
        def _():
            d = (z + s) * 2 + x
            arrived(t, d, c)
            pl.when(z > 0)(lambda: go(t, LEFT, d))
            go(t, ACROSS, d)
            go(t, OTHER, d)

    def across(t, s):
        @pl.when(z - s >= 0)
        def _():
            d = (z - s) * 2 + 1 - x
            arrived(t, d, c)
            go(t, OTHER, d)

        @pl.when((z + s < NZ) & (s > 0))
        def _():
            d = (z + s) * 2 + 1 - x
            arrived(t, d, c)
            go(t, OTHER, d)

    def sent(t):
        def body(d, _):
            zz, xx = d // 2, lax.rem(d, 2)

            @pl.when(xx == x)
            def _():
                pl.when((zz <= z) & (z < NZ - 1))(lambda: move(t, RIGHT, d).wait_send())
                pl.when((zz >= z) & (z > 0))(lambda: move(t, LEFT, d).wait_send())
                move(t, ACROSS, d).wait_send()

            pl.when(d != dp)(lambda: move(t, OTHER, d).wait_send())
            return 0

        lax.fori_loop(0, D, body, 0)

    start_own(0)
    start_own(1)

    def unit_dirs(ref):
        step = min(M, 512)
        for n in range(0, M, step):
            ref[n:n + step, :] = unit_rows(ref[n:n + step, :])

    loads[0].wait()
    unit_dirs(tdir)
    colv[...] = jnp.zeros_like(colv)

    def rows(i):
        return pl.ds(pl.multiple_of(i * R, R), R)

    def teach(i):
        a = tu[rows(i), :]
        for n in range(0, M, NC):
            e = jnp.exp2(by_rows(a, tdir[n:n + NC, :]) * (LOG2E / teacher_temp))
            expo[rows(i), n:n + NC] = e.astype(bf16)
            colv[:, n:n + NC] += jnp.sum(e, axis=0, keepdims=True)

    def teach_at(s):
        def body(k, _):
            zz = z + s * (2 * (k // 2) - 1)
            d = zz * 2 + lax.rem(x + lax.rem(k, 2), 2)
            ok = (zz >= 0) & (zz < NZ) & ((s > 0) | (k < 2))

            @pl.when(ok)
            def _():
                pl.when(d != dp)(lambda: arrived(0, d, 1 - c))
                teach(d)

            return 0

        lax.fori_loop(0, 4, body, 0)

    def gather_step(s, _):
        pl.when(s + 1 < NZ)(lambda: along(0, s + 1))
        across(0, s)
        teach_at(s)
        return 0

    lax.fori_loop(0, NZ, gather_step, 0)

    def place(i):
        return i // per, pl.multiple_of(lax.rem(i, per) * R, R)

    def row_pass(it):
        cs = split16(colv[...])

        def body(i, _):
            o = by_rows(cs, expo[rows(i), :])
            ci, off = place(i)
            rowp[it, ci, :, pl.ds(off, R)] = o[0:1] + o[1:2]
            return 0

        lax.fori_loop(0, D, body, 0)

    def col_pass(it):
        for i in range(D):
            off = (i % per) * R
            vec[i] = split16(1.0 / (B * fin[it, i // per, :, off:off + R]))

        def body(i, a):
            return a + jnp.dot(vec[i], expo[rows(i), :], preferred_element_type=f32)

        a = lax.fori_loop(0, D, body, jnp.zeros((16, M), f32))
        colv[...] = 1.0 / (protos * (a[0:1] + a[1:2]))

    def send(it, k, src, dst, dev):
        cp = pltpu.make_async_remote_copy(
            src_ref=src, dst_ref=dst, send_sem=asem.at[it, k], recv_sem=rsem.at[it, k],
            device_id=dev, device_id_type=MESH,
        )
        cp.start()
        return cp

    def all_reduce(it, values, first=None, second=None, third=None):
        n = values * C
        started = []
        for j in range(1, PS):
            p2, dev = plane(j)
            started.append(send(it, j - 1, rowp.at[it, p2, :, 0:n], b1.at[it, j - 1, :, 0:n], dev))
        if first is not None:
            first()
        for cp in started:
            cp.wait_recv()
        total = rowp[it, p, :, 0:n]
        for j in range(1, PS):
            total = total + b1[it, j - 1, :, 0:n]
        part[it, :, 0:n] = total
        ring = []
        for j in range(1, NZ):
            ring.append(send(it, PS - 2 + j, part.at[it, :, 0:n], b2.at[it, j - 1, :, 0:n], column(j)))
        if second is not None:
            second()
        for cp in ring:
            cp.wait_recv()
        for j in range(1, NZ):
            total = total + b2[it, j - 1, :, 0:n]
        fin[it, p, :, 0:n] = total
        last = []
        for j in range(1, PS):
            _, dev = plane(j)
            here = fin.at[it, p, :, 0:n]
            last.append(send(it, PS + NZ - 3 + j, here, here, dev))
        if third is not None:
            third()
        for j, cp in enumerate(last, 1):
            cp.wait_send()
            there = fin.at[it, lax.rem(p + PS - j, PS), :, 0:n]
            pltpu.make_async_remote_copy(
                src_ref=there, dst_ref=there, send_sem=asem.at[it, PS + NZ - 3 + j],
                recv_sem=rsem.at[it, PS + NZ - 3 + j], device_id=plane(j)[1], device_id_type=MESH,
            ).wait_recv()
        for cp in started + ring:
            cp.wait_send()

    def learn(i, _):
        pl.when(i != dp)(lambda: arrived(1, i, 1 - c))
        a = su[rows(i), :]
        ones = jnp.ones((16, NC), bf16)
        tot = jnp.zeros((16, R), f32)
        dot = jnp.zeros((16, R), f32)
        for n in range(0, M, NC):
            lg = by_rows(a, sdir[n:n + NC, :]) * (1.0 / student_temp)
            e = jnp.exp2(lg * LOG2E)
            eb = e.astype(bf16)
            expl[rows(i), n:n + NC] = eb
            tot = tot + by_rows(ones, eb)
            dot = dot + by_rows(ones, (e * lg).astype(bf16))
        ci, off = place(i)
        rowp[2, ci, :, pl.ds(off + C, R)] = tot[0:1]
        rowp[2, ci, :, pl.ds(off + 2 * C, R)] = dot[0:1]
        return 0

    def student_dirs():
        loads[1].wait()
        unit_dirs(sdir)

    def gather_rest():
        def body(s, _):
            pl.when(s + 1 < NZ)(lambda: along(1, s + 1))
            across(1, s)
            return 0

        lax.fori_loop(1, NZ, body, 0)

    def student():
        lax.fori_loop(0, D, learn, 0)

    colv[...] = 1.0 / (protos * colv[...])
    along(1, 1)
    across(1, 0)
    row_pass(0)
    all_reduce(0, 1, student_dirs, None, gather_rest)
    col_pass(0)
    row_pass(1)
    all_reduce(1, 1, student)
    col_pass(1)
    row_pass(2)
    all_reduce(2, 3)

    factor = protos / (B * student_temp)
    own, off = place(dp)
    stats[0:1, :] = fin[2, own, :, pl.ds(off + C, R)]
    stats[1:2, :] = fin[2, own, :, pl.ds(off + 2 * C, R)]
    acc[...] = jnp.zeros_like(acc)

    def grads(i, _):
        ci, off = place(i)
        rt = fin[2, ci, :, pl.ds(off, R)]
        tot = fin[2, ci, :, pl.ds(off + C, R)]
        row = lax.broadcasted_iota(jnp.int32, (8, R), 0)
        sides = jnp.where(row == 0, factor / tot, factor / rt).T
        pa, ra = sides[:, 0:1], sides[:, 1:2]
        for n in range(0, M, NC):
            e = expl[rows(i), n:n + NC].astype(f32)
            t = expo[rows(i), n:n + NC].astype(f32)
            dblk[:, n:n + NC] = (e * pa - (t * colv[:, n:n + NC]) * ra).astype(bf16)
        fterm[rows(i), :] = jnp.dot(dblk[...], sdir[...], preferred_element_type=f32)
        s = su[rows(i), :]
        for n in range(0, M, NC):
            acc[:, n:n + NC] += by_cols(s, dblk[:, n:n + NC])
        return 0

    lax.fori_loop(0, D, grads, 0)
    step = min(M, 256)
    for n in range(0, M, step):
        pg[n:n + step, :] = acc[:, n:n + step].T.astype(bf16)
    sent(0)
    sent(1)


def local(teacher_feat, student_feat, teacher_protos, student_protos):
    D, Q = lax.axis_size("dp"), lax.axis_size("proto")
    R, K = teacher_feat.shape
    M = teacher_protos.shape[0] // D
    B = D * R
    NZ, PS = D // 2, 2 * Q
    C = B // PS
    V = 3 * C
    hops = PS - 1 + NZ - 1 + PS - 1
    vmem = pl.BlockSpec(memory_space=pltpu.VMEM)
    hbm = pl.BlockSpec(memory_space=pl.ANY)
    stats, terms, proto_grad = pl.pallas_call(
        functools.partial(kernel, D, Q),
        out_shape=(
            jax.ShapeDtypeStruct((2, R), f32),
            jax.ShapeDtypeStruct((B, K), f32),
            jax.ShapeDtypeStruct((M, K), bf16),
        ),
        in_specs=[vmem, vmem, hbm, hbm],
        out_specs=(vmem, vmem, vmem),
        scratch_shapes=[
            pltpu.VMEM((M, K), bf16),
            pltpu.VMEM((M, K), bf16),
            pltpu.VMEM((B, K), bf16),
            pltpu.VMEM((B, K), bf16),
            pltpu.VMEM((B, M), bf16),
            pltpu.VMEM((B, M), bf16),
            pltpu.VMEM((R, M), bf16),
            pltpu.VMEM((K, M), f32),
            pltpu.VMEM((1, M), f32),
            pltpu.VMEM((D, 16, R), bf16),
            pltpu.VMEM((ITERS, PS, 1, V), f32),
            pltpu.VMEM((ITERS, 1, V), f32),
            pltpu.VMEM((ITERS, PS - 1, 1, V), f32),
            pltpu.VMEM((ITERS, NZ - 1, 1, V), f32),
            pltpu.VMEM((ITERS, PS, 1, V), f32),
            pltpu.SemaphoreType.DMA((2,)),
            pltpu.SemaphoreType.DMA((2, 4, D)),
            pltpu.SemaphoreType.DMA((2, D, 2)),
            pltpu.SemaphoreType.DMA((ITERS, hops)),
            pltpu.SemaphoreType.DMA((ITERS, hops)),
        ],
        compiler_params=pltpu.CompilerParams(
            collective_id=0, has_side_effects=True, vmem_limit_bytes=62 * 2**20
        ),
    )(teacher_feat, student_feat, teacher_protos, student_protos)
    factor = M * D * Q / (B * student_temp)
    grad = lax.psum_scatter(terms, "dp", scatter_dimension=0, tiled=True)
    grad = lax.psum(grad, "proto")
    unit = unit_rows(student_feat).astype(f32)
    cross = stats[1] / stats[0] - jnp.sum(unit * grad, axis=1) / (student_temp * factor)
    return jnp.log(stats[0]) - cross, grad.astype(bf16), proto_grad


def solution(mesh):
    placed = (P("dp", None), P("dp", None), P("proto", None), P("proto", None))
    return jax.shard_map(
        local,
        mesh=mesh,
        in_specs=placed,
        out_specs=(P("dp"), P("dp", None), P(("proto", "dp"), None)),
        check_vma=False,
    )
```

time: 484 us -> 255 us (0.53)
  blocking collectives: 179 us -> 0 us
  Pallas kernels: 0 us -> 114 us
  other arithmetic: 100 us -> 3.59 us
  matrix products: 66.2 us -> 0 us
    psum x5 -> x0, blocking collectives: 179 us -> none  [the longest x3 121 us: local(): row_total = lax.psum(jnp.sum(expo * col_scale[None, :], axis=1), both)]
    pallas_call x0 -> x1, Pallas kernels: none -> 114 us  [local(): pl.pallas_call(functools.partial(kernel, D, Q), out_shape=(jax.ShapeDtype...]
    dot_general x4 -> x0, matrix products: 66.2 us -> none  [the longest x2 43.8 us: by_rows(): lax.dot_general(left, right, (((1,), (1,)), ((), ())), preferred_element_...]
    reduce_sum x5 -> x0, other arithmetic: 62.9 us -> none  [the longest x3 38.4 us: local(): row_total = lax.psum(jnp.sum(expo * col_scale[None, :], axis=1), both)]
    all_gather x2 -> x0, waiting for transfers between devices: 46.4 us -> none  [the longest x1 46.4 us: local(): t_unit = lax.all_gather(unit_rows(teacher_feat), 'dp', tiled=True)]
    psum x0 -> x1, waiting for transfers between devices: none -> 34.7 us  [local(): grad = lax.psum(grad, 'proto')]
    convert_element_type x3 -> x1, other arithmetic: 31.1 us -> 2.09 us  [local(): return (jnp.log(stats[0]) - cross, grad.astype(bf16), proto_grad)]
    reduce_scatter x1, waiting for transfers between devices: 77.9 us -> 86.6 us  [local(): grad = lax.psum_scatter(terms, 'dp', scatter_dimension=0, tiled=True)]
  transfers between devices with their start and end apart: 3 -> 2, of which waited for: 2 -> 2; matrix products, arithmetic and copies ran while one was open for 20% -> 0% of each run, Pallas kernels for 0% -> 0%
where the time goes in v2:
time: 255 us
  waiting for transfers between devices  121 us (47%)
  Pallas kernels  114 us (45%)
  between operations  14.1 us (6%)
  other arithmetic  3.59 us (1%)
    pallas_call x1, Pallas kernels, local(): pl.pallas_call(functools.partial(kernel, D, Q), out_shape=(jax.ShapeDtype...  114 us
    reduce_scatter x1, waiting for transfers between devices, local(): grad = lax.psum_scatter(terms, 'dp', scatter_dimension=0, tiled=True)  86.6 us
    psum x1, waiting for transfers between devices, local(): grad = lax.psum(grad, 'proto')  34.7 us
  transfers between devices with their start and end apart: 2, of which 2 were waited for; matrix products, arithmetic and copies ran while one was open for 0% of the time, Pallas kernels for 0%

profile of v2, /device:TPU:0, one launch (start us, length us, event | category | flops | bytes accessed | tf_op | source)
XLA Modules:
  0.0 255.1 jit_solution(1320137503162829656)
XLA Ops:
  7.2 0.0 copy-start
  7.2 0.0 reduce-scatter.2.cloned.1.call-start
  7.2 113.8 %shard_map.67 = (f32[2,512]{1,0:T(2,128)}, f32[4096,256]{1,0:T(8,128)}, bf16[2048,256]{1,0:T(8,128)(2,1)}) custom-call(bf16[512,256]{1,0:T(8,128)(2,1)} %tf.1, bf16[512,256]{1,0:T(8,128)(2,1)} %sf.1, bf16[16384,256]{1,0:T(8,128)(2,1)} %tp.1, bf16[16384,256]{1,0:T(8,128)(2,1)} %sp.1), custom_call_target="tpu_custom_call" | custom-call | tf_op jit(solution)/shard_map/pallas_call | solution.py:367
  121.1 0.0 reduce-scatter.2.cloned.1.call-update
  121.1 0.0 all-reduce.2.cloned.1.call-start
  121.2 0.0 copy-done
  121.2 0.1 fusion
  121.3 86.6 %reduce-scatter.2.cloned.1.call-done = f32[512,256]{1,0:T(8,128)} async-done(((f32[4096,256]{1,0:T(8,128)}), f32[512,256]{1,0:T(8,128)}) %reduce-scatter.2.cloned.1.call-update) | async-done | bytes 524304 | tf_op jit(solution)/shard_map/reduce_scatter | solution.py:403
  207.9 0.0 all-reduce.2.cloned.1.call-update
  207.9 0.8 slice_divide_fusion
  208.7 34.7 %all-reduce.2.cloned.1.call-done = f32[512,256]{1,0:T(8,128)} async-done(((f32[512,256]{1,0:T(8,128)}), f32[512,256]{1,0:T(8,128)}) %all-reduce.2.cloned.1.call-update) | async-done | bytes 524304 | tf_op jit(solution)/shard_map/psum | solution.py:404
  243.3 2.1 fusion.2
  245.4 0.6 subtract_subtract_fusion
  246.0 2.3 copy.9
  (1 shorter events, 0.0 us)
Async XLA Ops:
  7.2 114.0 %copy-start = (bf16[512,256]{1,0:T(8,128)(2,1)S(1)}, bf16[512,256]{1,0:T(8,128)(2,1)}, u32[]{:S(2)}) copy-start(bf16[512,256]{1,0:T(8,128)(2,1)} %sf.1) | copy-start | bytes 786436
  7.2 200.7 %reduce-scatter.2.cloned.1.call-start = ((), (), s32[]{:S(2)}) async-start(), calls=%async_computation.1 | async-start | bytes 4718592 | tf_op jit(solution)/shard_map/reduce_scatter | solution.py:403
  121.1 122.2 %all-reduce.2.cloned.1.call-start = ((), (), s32[]{:S(2)}) async-start(), calls=%async_computation.2 | async-start | bytes 1048576 | tf_op jit(solution)/shard_map/psum | solution.py:404
Sparse Core Ops, SparseCore 0:
  121.2 86.5 reduce-scatter.1
  210.3 32.9 all-reduce.1

commit v3 on v2

--- a/solution.py
+++ b/solution.py
@@ -37,9 +37,10 @@
 
 
 def kernel(
-    D, Q, tf, sf, tp, sp, stats, fterm, pg,
-    tdir, sdir, tu, su, expo, expl, dblk, acc, colv, vec, rowp, part, b1, b2, fin,
-    load_sem, gs, gr, asem, rsem,
+    D, Q, tf, sf, tp, sp, stats, fg, pg,
+    tdir, sdir, tu, su, expo, expl, acc, colv, vec, rowp, part, b1, b2, fin,
+    terms, hold, s_c, r_c, s_xa, r_xa, s_yb, r_yb, s_ya, r_ya, s_xb, r_xb, s_z, r_z, own_z, r_g,
+    load_sem, gs, gr, asem, rsem, ssend, srecv,
 ):
     R, K = tf.shape
     M = tdir.shape[0]
@@ -327,28 +328,177 @@
     stats[0:1, :] = fin[2, own, :, pl.ds(off + C, R)]
     stats[1:2, :] = fin[2, own, :, pl.ds(off + 2 * C, R)]
     acc[...] = jnp.zeros_like(acc)
-
-    def grads(i, _):
+    NY = Q // 2
+    y = q // 2
+    HA = H // 2
+    PA = HA // NY
+    to_core = {"dp": dp, "proto": core}
+    to_x = {"dp": z * 2 + 1 - x, "proto": q}
+    C0, XA, YB, YA, XB, Z0, G0 = 0, D, D + NZ, D + NZ * NY, D + NZ * (2 * NY - 1), D + 2 * NZ * NY, D + NZ * (2 * NY + 1)
+
+    def to_y(j):
+        y2 = lax.rem(y + j, NY)
+        return y2, {"dp": dp, "proto": y2 * 2 + c}
+
+    def hop(k, src, dst, dev):
+        return pltpu.make_async_remote_copy(
+            src_ref=src, dst_ref=dst, send_sem=ssend.at[k], recv_sem=srecv.at[k],
+            device_id=dev, device_id_type=MESH,
+        )
+
+    def hop_core(i):
+        return hop(C0 + i, s_c.at[i], r_c.at[i], to_core)
+
+    def hop_xa(zz):
+        return hop(XA + zz, s_xa.at[zz], r_xa.at[zz], to_x)
+
+    def hop_yb(zz, j):
+        return hop(YB + zz * (NY - 1) + j - 1, s_yb.at[zz, j - 1], r_yb.at[zz, j - 1], to_y(j)[1])
+
+    def hop_ya(zz, j):
+        return hop(YA + zz * (NY - 1) + j - 1, s_ya.at[zz, j - 1], r_ya.at[zz, j - 1], to_y(j)[1])
+
+    def hop_xb(zz):
+        return hop(XB + zz, s_xb.at[zz], r_xb.at[zz], to_x)
+
+    def hop_z(j):
+        return hop(Z0 + j - 1, s_z.at[j - 1], r_z.at[j - 1], column(j))
+
+    def hop_g(j, slot):
+        return hop(G0 + j - 1, r_g.at[slot], r_g.at[slot], {"dp": dp, "proto": lax.rem(q + j, Q)})
+
+    def grads(i):
         ci, off = place(i)
         rt = fin[2, ci, :, pl.ds(off, R)]
         tot = fin[2, ci, :, pl.ds(off + C, R)]
         row = lax.broadcasted_iota(jnp.int32, (8, R), 0)
         sides = jnp.where(row == 0, factor / tot, factor / rt).T
         pa, ra = sides[:, 0:1], sides[:, 1:2]
+        total = jnp.zeros((R, K), f32)
         for n in range(0, M, NC):
             e = expl[rows(i), n:n + NC].astype(f32)
             t = expo[rows(i), n:n + NC].astype(f32)
-            dblk[:, n:n + NC] = (e * pa - (t * colv[:, n:n + NC]) * ra).astype(bf16)
-        fterm[rows(i), :] = jnp.dot(dblk[...], sdir[...], preferred_element_type=f32)
-        s = su[rows(i), :]
-        for n in range(0, M, NC):
-            acc[:, n:n + NC] += by_cols(s, dblk[:, n:n + NC])
+            d = (e * pa - (t * colv[:, n:n + NC]) * ra).astype(bf16)
+            expl[rows(i), n:n + NC] = d
+            total = total + jnp.dot(d, sdir[n:n + NC, :], preferred_element_type=f32)
+        terms[...] = total
+        hold[i] = terms[pl.ds(pl.multiple_of(c * H, H), H), :]
+        s_c[i] = terms[pl.ds(pl.multiple_of((1 - c) * H, H), H), :].astype(bf16)
+        hop_core(i).start()
+
+    def piece(k, base):
+        return pl.ds(pl.multiple_of(base + k * PA, PA), PA)
+
+    def stage1(zz):
+        for xx in range(2):
+            i = zz * 2 + xx
+            hop_core(i).wait_recv()
+            hold[i] = hold[i] + r_c[i].astype(f32)
+        s_xa[zz] = hold[zz * 2 + 1 - x, 0:HA, :].astype(bf16)
+        hop_xa(zz).start()
+        for j in range(1, NY):
+            y2, _ = to_y(j)
+            for xx in range(2):
+                s_yb[zz, j - 1, xx] = hold[zz * 2 + xx, piece(y2, HA), :].astype(bf16)
+            hop_yb(zz, j).start()
+
+    def stage2(zz):
+        mine, other = zz * 2 + x, zz * 2 + 1 - x
+        hop_xa(zz).wait_recv()
+        hold[mine, 0:HA, :] = hold[mine, 0:HA, :] + r_xa[zz].astype(f32)
+        for j in range(1, NY):
+            y2, _ = to_y(j)
+            s_ya[zz, j - 1] = hold[mine, piece(y2, 0), :].astype(bf16)
+            hop_ya(zz, j).start()
+        for j in range(1, NY):
+            hop_yb(zz, j).wait_recv()
+            for xx in range(2):
+                at = piece(y, HA)
+                hold[zz * 2 + xx, at, :] = hold[zz * 2 + xx, at, :] + r_yb[zz, j - 1, xx].astype(f32)
+        s_xb[zz] = hold[other, piece(y, HA), :].astype(bf16)
+        hop_xb(zz).start()
+
+    def stage3(zz):
+        mine = zz * 2 + x
+        first, second = hold[mine, piece(y, 0), :], hold[mine, piece(y, HA), :]
+        for j in range(1, NY):
+            hop_ya(zz, j).wait_recv()
+            first = first + r_ya[zz, j - 1].astype(f32)
+        hop_xb(zz).wait_recv()
+        second = second + r_xb[zz].astype(f32)
+
+        @pl.when(zz == z)
+        def _():
+            own_z[0:PA, :] = first
+            own_z[PA:2 * PA, :] = second
+
+        for j in range(1, NZ):
+            @pl.when(lax.rem(z + j, NZ) == zz)
+            def _():
+                s_z[j - 1, 0:PA, :] = first.astype(bf16)
+                s_z[j - 1, PA:2 * PA, :] = second.astype(bf16)
+                hop_z(j).start()
+
+    def grad_step(t, _):
+        grads(2 * t)
+        grads(2 * t + 1)
+        pl.when(t >= 1)(lambda: stage1(t - 1))
+        pl.when(t >= 2)(lambda: stage2(t - 2))
+        pl.when(t >= 3)(lambda: stage3(t - 3))
         return 0
 
-    lax.fori_loop(0, D, grads, 0)
-    step = min(M, 256)
-    for n in range(0, M, step):
-        pg[n:n + step, :] = acc[:, n:n + step].T.astype(bf16)
+    lax.fori_loop(0, NZ, grad_step, 0)
+
+    def protos_of(k):
+        def body(i, _):
+            s = su[rows(i), :]
+            for n in range(0, M, NC):
+                acc[:, n:n + NC] += by_cols(s, expl[rows(i), n:n + NC])
+            return 0
+
+        lax.fori_loop(k * D // 4, (k + 1) * D // 4, body, 0)
+
+    stage1(NZ - 1)
+    stage2(NZ - 2)
+    stage3(NZ - 3)
+    protos_of(0)
+    stage2(NZ - 1)
+    stage3(NZ - 2)
+    protos_of(1)
+    stage3(NZ - 1)
+    protos_of(2)
+    total = own_z[...]
+    for j in range(1, NZ):
+        hop_z(j).wait_recv()
+        total = total + r_z[j - 1].astype(f32)
+    r_g[q] = total.astype(bf16)
+    for j in range(1, Q):
+        hop_g(j, q).start()
+    protos_of(3)
+    chunk = min(M, 256)
+    for n in range(0, M, chunk):
+        pg[n:n + chunk, :] = acc[:, n:n + chunk].T.astype(bf16)
+    for j in range(1, Q):
+        hop_g(j, q).wait_send()
+        hop_g(j, lax.rem(q + Q - j, Q)).wait_recv()
+    for k in range(Q):
+        base = (k % 2) * H + (k // 2) * PA
+        fg[base:base + PA, :] = r_g[k, 0:PA, :]
+        fg[base + HA:base + HA + PA, :] = r_g[k, PA:2 * PA, :]
+
+    def flushed(zz, _):
+        hop_core(zz * 2).wait_send()
+        hop_core(zz * 2 + 1).wait_send()
+        hop_xa(zz).wait_send()
+        hop_xb(zz).wait_send()
+        for j in range(1, NY):
+            hop_yb(zz, j).wait_send()
+            hop_ya(zz, j).wait_send()
+        return 0
+
+    lax.fori_loop(0, NZ, flushed, 0)
+    for j in range(1, NZ):
+        hop_z(j).wait_send()
     sent(0)
     sent(1)
 
@@ -364,11 +514,16 @@
     hops = PS - 1 + NZ - 1 + PS - 1
     vmem = pl.BlockSpec(memory_space=pltpu.VMEM)
     hbm = pl.BlockSpec(memory_space=pl.ANY)
-    stats, terms, proto_grad = pl.pallas_call(
+    NY = Q // 2
+    H = R // 2
+    HA = H // 2
+    PA = HA // NY
+    waits = D + NZ * (2 * NY + 1) + Q - 1
+    stats, grad, proto_grad = pl.pallas_call(
         functools.partial(kernel, D, Q),
         out_shape=(
             jax.ShapeDtypeStruct((2, R), f32),
-            jax.ShapeDtypeStruct((B, K), f32),
+            jax.ShapeDtypeStruct((R, K), bf16),
             jax.ShapeDtypeStruct((M, K), bf16),
         ),
         in_specs=[vmem, vmem, hbm, hbm],
@@ -380,7 +535,6 @@
             pltpu.VMEM((B, K), bf16),
             pltpu.VMEM((B, M), bf16),
             pltpu.VMEM((B, M), bf16),
-            pltpu.VMEM((R, M), bf16),
             pltpu.VMEM((K, M), f32),
             pltpu.VMEM((1, M), f32),
             pltpu.VMEM((D, 16, R), bf16),
@@ -389,22 +543,38 @@
             pltpu.VMEM((ITERS, PS - 1, 1, V), f32),
             pltpu.VMEM((ITERS, NZ - 1, 1, V), f32),
             pltpu.VMEM((ITERS, PS, 1, V), f32),
+            pltpu.VMEM((R, K), f32),
+            pltpu.VMEM((D, H, K), f32),
+            pltpu.VMEM((D, H, K), bf16),
+            pltpu.VMEM((D, H, K), bf16),
+            pltpu.VMEM((NZ, HA, K), bf16),
+            pltpu.VMEM((NZ, HA, K), bf16),
+            pltpu.VMEM((NZ, NY - 1, 2, PA, K), bf16),
+            pltpu.VMEM((NZ, NY - 1, 2, PA, K), bf16),
+            pltpu.VMEM((NZ, NY - 1, PA, K), bf16),
+            pltpu.VMEM((NZ, NY - 1, PA, K), bf16),
+            pltpu.VMEM((NZ, PA, K), bf16),
+            pltpu.VMEM((NZ, PA, K), bf16),
+            pltpu.VMEM((NZ - 1, 2 * PA, K), bf16),
+            pltpu.VMEM((NZ - 1, 2 * PA, K), bf16),
+            pltpu.VMEM((2 * PA, K), f32),
+            pltpu.VMEM((Q, 2 * PA, K), bf16),
             pltpu.SemaphoreType.DMA((2,)),
             pltpu.SemaphoreType.DMA((2, 4, D)),
             pltpu.SemaphoreType.DMA((2, D, 2)),
             pltpu.SemaphoreType.DMA((ITERS, hops)),
             pltpu.SemaphoreType.DMA((ITERS, hops)),
+            pltpu.SemaphoreType.DMA((waits,)),
+            pltpu.SemaphoreType.DMA((waits,)),
         ],
         compiler_params=pltpu.CompilerParams(
             collective_id=0, has_side_effects=True, vmem_limit_bytes=62 * 2**20
         ),
     )(teacher_feat, student_feat, teacher_protos, student_protos)
     factor = M * D * Q / (B * student_temp)
-    grad = lax.psum_scatter(terms, "dp", scatter_dimension=0, tiled=True)
-    grad = lax.psum(grad, "proto")
     unit = unit_rows(student_feat).astype(f32)
-    cross = stats[1] / stats[0] - jnp.sum(unit * grad, axis=1) / (student_temp * factor)
-    return jnp.log(stats[0]) - cross, grad.astype(bf16), proto_grad
+    cross = stats[1] / stats[0] - jnp.sum(unit * grad.astype(f32), axis=1) / (student_temp * factor)
+    return jnp.log(stats[0]) - cross, grad, proto_grad
 
 
 def solution(mesh):

time: 255 us -> 137 us (0.54)
  waiting for transfers between devices: 121 us -> 0 us
  Pallas kernels: 114 us -> 128 us
  between operations: 14.1 us -> 0.67 us
    reduce_scatter x1 -> x0, waiting for transfers between devices: 86.6 us -> none  [local(): grad = lax.psum_scatter(terms, 'dp', scatter_dimension=0, tiled=True)]
    psum x1 -> x0, waiting for transfers between devices: 34.7 us -> none  [local(): grad = lax.psum(grad, 'proto')]
    pallas_call x1, Pallas kernels: 114 us -> 128 us  [local(): pl.pallas_call(functools.partial(kernel, D, Q), out_shape=(jax.ShapeDtype...]
  transfers between devices with their start and end apart: 2 -> 0, of which waited for: 2 -> 0; matrix products, arithmetic and copies ran while one was open for 0% -> 0% of each run, Pallas kernels for 0% -> 0%
where the time goes in v3:
time: 137 us; the launch traced here: 136 us
  Pallas kernels  128 us (93%)
  local copies, waits for them, and re-layouts  3.94 us (3%)
  other arithmetic  3.64 us (3%)
    pallas_call x1, Pallas kernels, local(): pl.pallas_call(functools.partial(kernel, D, Q), out_shape=(jax.ShapeDtype...  128 us
    unnamed x4, local copies, waits for them, and re-layouts  3.94 us

profile of v3, /device:TPU:0, one launch (start us, length us, event | category | flops | bytes accessed | tf_op | source)
XLA Modules:
  0.0 136.5 jit_solution(15264217028586516187)
XLA Ops:
  0.6 1.1 fusion
  1.7 0.0 copy-start
  1.8 128.3 %shard_map.67 = (f32[2,512]{1,0:T(2,128)}, bf16[512,256]{1,0:T(8,128)(2,1)}, bf16[2048,256]{1,0:T(8,128)(2,1)}) custom-call(bf16[512,256]{1,0:T(8,128)(2,1)} %tf.1, bf16[512,256]{1,0:T(8,128)(2,1)} %sf.1, bf16[16384,256]{1,0:T(8,128)(2,1)} %tp.1, bf16[16384,256]{1,0:T(8,128)(2,1)} %sp.1), custom_call_target="tpu_custom_call" | custom-call | tf_op jit(solution)/shard_map/pallas_call | solution.py:522
  130.0 0.0 copy-done
  130.0 1.2 multiply_reduce_fusion
  131.2 0.8 slice_divide_fusion
  132.0 0.6 subtract_subtract_fusion
  132.6 1.7 %copy.9 = bf16[512,256]{1,0:T(8,128)(2,1)} copy(bf16[512,256]{1,0:T(8,128)(2,1)} %get-tuple-element.15) | data formatting | bytes 524288
  134.2 2.3 %copy.10 = bf16[2048,256]{1,0:T(8,128)(2,1)} copy(bf16[2048,256]{1,0:T(8,128)(2,1)} %get-tuple-element.16) | data formatting | bytes 2097152
  (1 shorter events, 0.0 us)
Async XLA Ops:
  1.7 128.3 %copy-start = (bf16[512,256]{1,0:T(8,128)(2,1)S(1)}, bf16[512,256]{1,0:T(8,128)(2,1)}, u32[]{:S(2)}) copy-start(bf16[512,256]{1,0:T(8,128)(2,1)} %sf.1) | copy-start | bytes 786436

commit v4 on v3

--- a/solution.py
+++ b/solution.py
@@ -21,14 +21,6 @@
     return (xf * lax.rsqrt(jnp.sum(xf * xf, axis=1, keepdims=True) + 1e-06)).astype(bf16)
 
 
-def by_rows(left, right):
-    return lax.dot_general(left, right, (((1,), (1,)), ((), ())), preferred_element_type=f32)
-
-
-def by_cols(left, right):
-    return lax.dot_general(left, right, (((0,), (0,)), ((), ())), preferred_element_type=f32)
-
-
 def split16(x):
     n = x.shape[1]
     hi = x.astype(bf16).astype(f32)
@@ -38,8 +30,8 @@
 
 def kernel(
     D, Q, tf, sf, tp, sp, stats, fg, pg,
-    tdir, sdir, tu, su, expo, expl, acc, colv, vec, rowp, part, b1, b2, fin,
-    terms, hold, s_c, r_c, s_xa, r_xa, s_yb, r_yb, s_ya, r_ya, s_xb, r_xb, s_z, r_z, own_z, r_g,
+    tdir, sdir, tdir_t, sdir_t, sum_a, sum_b, tu, su, expo, expl, acc, colv, vec, rowp, part, b1, b2, fin,
+    terms, hold, r_c, s_xa, r_xa, s_yb, r_yb, s_ya, r_ya, s_xb, r_xb, s_z, r_z, own_z, r_g,
     load_sem, gs, gr, asem, rsem, ssend, srecv,
 ):
     R, K = tf.shape
@@ -160,15 +152,16 @@
         lax.fori_loop(0, D, body, 0)
 
     start_own(0)
-    start_own(1)
-
-    def unit_dirs(ref):
-        step = min(M, 512)
+
+    def unit_dirs(ref, turned):
+        step = min(M, 256)
         for n in range(0, M, step):
-            ref[n:n + step, :] = unit_rows(ref[n:n + step, :])
+            u = unit_rows(ref[n:n + step, :])
+            ref[n:n + step, :] = u
+            turned[:, n:n + step] = u.astype(f32).T.astype(bf16)
 
     loads[0].wait()
-    unit_dirs(tdir)
+    unit_dirs(tdir, tdir_t)
     colv[...] = jnp.zeros_like(colv)
 
     def rows(i):
@@ -177,7 +170,8 @@
     def teach(i):
         a = tu[rows(i), :]
         for n in range(0, M, NC):
-            e = jnp.exp2(by_rows(a, tdir[n:n + NC, :]) * (LOG2E / teacher_temp))
+            t = jnp.dot(a, tdir_t[:, n:n + NC], preferred_element_type=f32)
+            e = jnp.exp2(t * (LOG2E / teacher_temp))
             expo[rows(i), n:n + NC] = e.astype(bf16)
             colv[:, n:n + NC] += jnp.sum(e, axis=0, keepdims=True)
 
@@ -199,6 +193,7 @@
     def gather_step(s, _):
         pl.when(s + 1 < NZ)(lambda: along(0, s + 1))
         across(0, s)
+        pl.when(s == 1)(lambda: start_own(1))
         teach_at(s)
         return 0
 
@@ -207,13 +202,19 @@
     def place(i):
         return i // per, pl.multiple_of(lax.rem(i, per) * R, R)
 
+    def lanes_to_row(ref):
+        return jnp.sum(ref[...].T, axis=0, keepdims=True)
+
     def row_pass(it):
-        cs = split16(colv[...])
-
         def body(i, _):
-            o = by_rows(cs, expo[rows(i), :])
+            for r in range(0, R, 128):
+                at = pl.ds(pl.multiple_of(i * R + r, 128), 128)
+                total = jnp.zeros((128, 128), f32)
+                for n in range(0, M, 128):
+                    total = total + expo[at, n:n + 128].astype(f32) * colv[:, n:n + 128]
+                sum_a[r:r + 128, :] = total
             ci, off = place(i)
-            rowp[it, ci, :, pl.ds(off, R)] = o[0:1] + o[1:2]
+            rowp[it, ci, :, pl.ds(off, R)] = lanes_to_row(sum_a)
             return 0
 
         lax.fori_loop(0, D, body, 0)
@@ -281,24 +282,26 @@
     def learn(i, _):
         pl.when(i != dp)(lambda: arrived(1, i, 1 - c))
         a = su[rows(i), :]
-        ones = jnp.ones((16, NC), bf16)
-        tot = jnp.zeros((16, R), f32)
-        dot = jnp.zeros((16, R), f32)
         for n in range(0, M, NC):
-            lg = by_rows(a, sdir[n:n + NC, :]) * (1.0 / student_temp)
-            e = jnp.exp2(lg * LOG2E)
-            eb = e.astype(bf16)
-            expl[rows(i), n:n + NC] = eb
-            tot = tot + by_rows(ones, eb)
-            dot = dot + by_rows(ones, (e * lg).astype(bf16))
+            t = jnp.dot(a, sdir_t[:, n:n + NC], preferred_element_type=f32)
+            e = jnp.exp2(t * (LOG2E / student_temp))
+            expl[rows(i), n:n + NC] = e.astype(bf16)
+            w = e * t
+            ea, wa = e[:, 0:128], w[:, 0:128]
+            for k in range(128, NC, 128):
+                ea, wa = ea + e[:, k:k + 128], wa + w[:, k:k + 128]
+            sum_a[...] = ea if n == 0 else sum_a[...] + ea
+            sum_b[...] = wa if n == 0 else sum_b[...] + wa
         ci, off = place(i)
-        rowp[2, ci, :, pl.ds(off + C, R)] = tot[0:1]
-        rowp[2, ci, :, pl.ds(off + 2 * C, R)] = dot[0:1]
+        rowp[2, ci, :, pl.ds(off + C, R)] = lanes_to_row(sum_a)
+        rowp[2, ci, :, pl.ds(off + 2 * C, R)] = lanes_to_row(sum_b) * (1.0 / student_temp)
         return 0
 
     def student_dirs():
+        along(1, 1)
+        across(1, 0)
         loads[1].wait()
-        unit_dirs(sdir)
+        unit_dirs(sdir, sdir_t)
 
     def gather_rest():
         def body(s, _):
@@ -308,20 +311,18 @@
 
         lax.fori_loop(1, NZ, body, 0)
 
-    def student():
-        lax.fori_loop(0, D, learn, 0)
+    def student(k):
+        return lambda: lax.fori_loop(k * D // 3, (k + 1) * D // 3, learn, 0)
 
     colv[...] = 1.0 / (protos * colv[...])
-    along(1, 1)
-    across(1, 0)
     row_pass(0)
     all_reduce(0, 1, student_dirs, None, gather_rest)
     col_pass(0)
     row_pass(1)
-    all_reduce(1, 1, student)
+    all_reduce(1, 1, student(0), student(1), student(2))
     col_pass(1)
     row_pass(2)
-    all_reduce(2, 3)
+    all_reduce(2, 3, lambda: sent(0))
 
     factor = protos / (B * student_temp)
     own, off = place(dp)
@@ -347,7 +348,7 @@
         )
 
     def hop_core(i):
-        return hop(C0 + i, s_c.at[i], r_c.at[i], to_core)
+        return hop(C0 + i, half(0, i, 0), r_c.at[i], to_core)
 
     def hop_xa(zz):
         return hop(XA + zz, s_xa.at[zz], r_xa.at[zz], to_x)
@@ -383,7 +384,7 @@
             total = total + jnp.dot(d, sdir[n:n + NC, :], preferred_element_type=f32)
         terms[...] = total
         hold[i] = terms[pl.ds(pl.multiple_of(c * H, H), H), :]
-        s_c[i] = terms[pl.ds(pl.multiple_of((1 - c) * H, H), H), :].astype(bf16)
+        tu[pl.ds(pl.multiple_of(i * R, R), H), :] = terms[pl.ds(pl.multiple_of((1 - c) * H, H), H), :].astype(bf16)
         hop_core(i).start()
 
     def piece(k, base):
@@ -451,9 +452,9 @@
 
     def protos_of(k):
         def body(i, _):
-            s = su[rows(i), :]
+            s = su[rows(i), :].astype(f32).T.astype(bf16)
             for n in range(0, M, NC):
-                acc[:, n:n + NC] += by_cols(s, expl[rows(i), n:n + NC])
+                acc[:, n:n + NC] += jnp.dot(s, expl[rows(i), n:n + NC], preferred_element_type=f32)
             return 0
 
         lax.fori_loop(k * D // 4, (k + 1) * D // 4, body, 0)
@@ -499,7 +500,6 @@
     lax.fori_loop(0, NZ, flushed, 0)
     for j in range(1, NZ):
         hop_z(j).wait_send()
-    sent(0)
     sent(1)
 
 
@@ -531,6 +531,10 @@
         scratch_shapes=[
             pltpu.VMEM((M, K), bf16),
             pltpu.VMEM((M, K), bf16),
+            pltpu.VMEM((K, M), bf16),
+            pltpu.VMEM((K, M), bf16),
+            pltpu.VMEM((R, 128), f32),
+            pltpu.VMEM((R, 128), f32),
             pltpu.VMEM((B, K), bf16),
             pltpu.VMEM((B, K), bf16),
             pltpu.VMEM((B, M), bf16),
@@ -545,7 +549,6 @@
             pltpu.VMEM((ITERS, PS, 1, V), f32),
             pltpu.VMEM((R, K), f32),
             pltpu.VMEM((D, H, K), f32),
-            pltpu.VMEM((D, H, K), bf16),
             pltpu.VMEM((D, H, K), bf16),
             pltpu.VMEM((NZ, HA, K), bf16),
             pltpu.VMEM((NZ, HA, K), bf16),

time: 137 us -> 119 us (0.87)
  Pallas kernels: 128 us -> 110 us
    pallas_call x1, Pallas kernels: 128 us -> 110 us  [local(): pl.pallas_call(functools.partial(kernel, D, Q), out_shape=(jax.ShapeDtype...]
where the time goes in v4:
time: 119 us; the launch traced here: 118 us
  Pallas kernels  110 us (92%)
  local copies, waits for them, and re-layouts  3.94 us (3%)
  other arithmetic  3.64 us (3%)
    pallas_call x1, Pallas kernels, local(): pl.pallas_call(functools.partial(kernel, D, Q), out_shape=(jax.ShapeDtype...  110 us
    unnamed x4, local copies, waits for them, and re-layouts  3.94 us

profile of v4, /device:TPU:0, one launch (start us, length us, event | category | flops | bytes accessed | tf_op | source)
XLA Modules:
  0.0 118.2 jit_solution(1593135397508910458)
XLA Ops:
  0.6 1.1 fusion
  1.7 0.0 copy-start
  1.8 110.0 %shard_map.67 = (f32[2,512]{1,0:T(2,128)}, bf16[512,256]{1,0:T(8,128)(2,1)}, bf16[2048,256]{1,0:T(8,128)(2,1)}) custom-call(bf16[512,256]{1,0:T(8,128)(2,1)} %tf.1, bf16[512,256]{1,0:T(8,128)(2,1)} %sf.1, bf16[16384,256]{1,0:T(8,128)(2,1)} %tp.1, bf16[16384,256]{1,0:T(8,128)(2,1)} %sp.1), custom_call_target="tpu_custom_call" | custom-call | tf_op jit(solution)/shard_map/pallas_call | solution.py:522
  111.7 0.0 copy-done
  111.7 1.2 %multiply_reduce_fusion = f32[512]{0:T(512)S(1)} fusion(bf16[512,256]{1,0:T(8,128)(2,1)} %get-tuple-element.15, bf16[512,256]{1,0:T(8,128)(2,1)S(1)} %copy-done, f32[512]{0:T(512)S(1)} %add_rsqrt_fusion), kind=kLoop, calls=%fused_computation.4 | loop fusion | flops 916992 | bytes 528384 | tf_op jit(solution)/shard_map/reduce_sum | solution.py:579
  112.9 0.8 slice_divide_fusion
  113.7 0.6 subtract_subtract_fusion
  114.3 1.7 %copy.9 = bf16[512,256]{1,0:T(8,128)(2,1)} copy(bf16[512,256]{1,0:T(8,128)(2,1)} %get-tuple-element.15) | data formatting | bytes 524288
  116.0 2.3 %copy.10 = bf16[2048,256]{1,0:T(8,128)(2,1)} copy(bf16[2048,256]{1,0:T(8,128)(2,1)} %get-tuple-element.16) | data formatting | bytes 2097152
  (1 shorter events, 0.0 us)
Async XLA Ops:
  1.7 110.0 %copy-start = (bf16[512,256]{1,0:T(8,128)(2,1)S(1)}, bf16[512,256]{1,0:T(8,128)(2,1)}, u32[]{:S(2)}) copy-start(bf16[512,256]{1,0:T(8,128)(2,1)} %sf.1) | copy-start | bytes 786436

commit v5 on v4

--- a/solution.py
+++ b/solution.py
@@ -21,16 +21,9 @@
     return (xf * lax.rsqrt(jnp.sum(xf * xf, axis=1, keepdims=True) + 1e-06)).astype(bf16)
 
 
-def split16(x):
-    n = x.shape[1]
-    hi = x.astype(bf16).astype(f32)
-    row = lax.broadcasted_iota(jnp.int32, (16, n), 0)
-    return jnp.where(row == 0, hi, jnp.where(row == 1, x - hi, 0.0)).astype(bf16)
-
-
 def kernel(
-    D, Q, tf, sf, tp, sp, stats, fg, pg,
-    tdir, sdir, tdir_t, sdir_t, sum_a, sum_b, tu, su, expo, expl, acc, colv, vec, rowp, part, b1, b2, fin,
+    D, Q, tf, sf, tp, sp, loss, fg, pg,
+    tdir, sdir, tdir_t, sdir_t, sum_a, sum_b, tu, su, expo, expl, acc, colv, rowp, part, b1, b2, fin,
     terms, hold, r_c, s_xa, r_xa, s_yb, r_yb, s_ya, r_ya, s_xb, r_xb, s_z, r_z, own_z, r_g,
     load_sem, gs, gr, asem, rsem, ssend, srecv,
 ):
@@ -220,15 +213,23 @@
         lax.fori_loop(0, D, body, 0)
 
     def col_pass(it):
-        for i in range(D):
-            off = (i % per) * R
-            vec[i] = split16(1.0 / (B * fin[it, i // per, :, off:off + R]))
-
-        def body(i, a):
-            return a + jnp.dot(vec[i], expo[rows(i), :], preferred_element_type=f32)
-
-        a = lax.fori_loop(0, D, body, jnp.zeros((16, M), f32))
-        colv[...] = 1.0 / (protos * (a[0:1] + a[1:2]))
+        colv[...] = jnp.zeros_like(colv)
+
+        def body(i, _):
+            ci, off = place(i)
+            scale = 1.0 / (B * fin[it, ci, :, pl.ds(off, R)])
+            sum_a[...] = jnp.broadcast_to(jnp.broadcast_to(scale, (8, R)).T[:, 0:1], (R, 128))
+            for n in range(0, M, 128):
+                total = jnp.zeros((8, 128), f32)
+                for r in range(0, R, 128):
+                    at = pl.ds(pl.multiple_of(i * R + r, 128), 128)
+                    w = expo[at, n:n + 128].astype(f32) * sum_a[r:r + 128, :]
+                    total = total + jnp.sum(w.reshape(16, 8, 128), axis=0)
+                colv[:, n:n + 128] += jnp.sum(total, axis=0, keepdims=True)
+            return 0
+
+        lax.fori_loop(0, D, body, 0)
+        colv[...] = 1.0 / (protos * colv[...])
 
     def send(it, k, src, dst, dev):
         cp = pltpu.make_async_remote_copy(
@@ -325,9 +326,6 @@
     all_reduce(2, 3, lambda: sent(0))
 
     factor = protos / (B * student_temp)
-    own, off = place(dp)
-    stats[0:1, :] = fin[2, own, :, pl.ds(off + C, R)]
-    stats[1:2, :] = fin[2, own, :, pl.ds(off + 2 * C, R)]
     acc[...] = jnp.zeros_like(acc)
     NY = Q // 2
     y = q // 2
@@ -487,6 +485,15 @@
         fg[base:base + PA, :] = r_g[k, 0:PA, :]
         fg[base + HA:base + HA + PA, :] = r_g[k, PA:2 * PA, :]
 
+    w = su[rows(dp), :].astype(f32) * fg[...].astype(f32)
+    sum_a[...] = w[:, 0:128]
+    for k in range(128, K, 128):
+        sum_a[...] += w[:, k:k + 128]
+    own, off = place(dp)
+    tot = fin[2, own, :, pl.ds(off + C, R)]
+    mean = fin[2, own, :, pl.ds(off + 2 * C, R)] / tot
+    loss[...] = jnp.log(tot) - (mean - lanes_to_row(sum_a) * (1.0 / (student_temp * factor)))
+
     def flushed(zz, _):
         hop_core(zz * 2).wait_send()
         hop_core(zz * 2 + 1).wait_send()
@@ -519,10 +526,10 @@
     HA = H // 2
     PA = HA // NY
     waits = D + NZ * (2 * NY + 1) + Q - 1
-    stats, grad, proto_grad = pl.pallas_call(
+    loss, grad, proto_grad = pl.pallas_call(
         functools.partial(kernel, D, Q),
         out_shape=(
-            jax.ShapeDtypeStruct((2, R), f32),
+            jax.ShapeDtypeStruct((1, R), f32),
             jax.ShapeDtypeStruct((R, K), bf16),
             jax.ShapeDtypeStruct((M, K), bf16),
         ),
@@ -541,7 +548,6 @@
             pltpu.VMEM((B, M), bf16),
             pltpu.VMEM((K, M), f32),
             pltpu.VMEM((1, M), f32),
-            pltpu.VMEM((D, 16, R), bf16),
             pltpu.VMEM((ITERS, PS, 1, V), f32),
             pltpu.VMEM((ITERS, 1, V), f32),
             pltpu.VMEM((ITERS, PS - 1, 1, V), f32),
@@ -574,10 +580,7 @@
             collective_id=0, has_side_effects=True, vmem_limit_bytes=62 * 2**20
         ),
     )(teacher_feat, student_feat, teacher_protos, student_protos)
-    factor = M * D * Q / (B * student_temp)
-    unit = unit_rows(student_feat).astype(f32)
-    cross = stats[1] / stats[0] - jnp.sum(unit * grad.astype(f32), axis=1) / (student_temp * factor)
-    return jnp.log(stats[0]) - cross, grad, proto_grad
+    return loss.reshape(R), grad, proto_grad
 
 
 def solution(mesh):

time: 119 us -> 120 us (level)
  other arithmetic: 3.64 us -> 0 us
  Pallas kernels: 110 us -> 113 us
  local copies, waits for them, and re-layouts: 3.94 us -> 5.18 us
    pallas_call x1, Pallas kernels: 110 us -> 113 us  [local(): pl.pallas_call(functools.partial(kernel, D, Q), out_shape=(jax.ShapeDtype...]
    reduce_sum x2 -> x0, other arithmetic: 2.29 us -> none  [the longest x1 1.19 us: local(): jnp.sum(unit * grad.astype(f32), axis=1) / (student_temp * factor)]
    unnamed x4 -> x3, local copies, waits for them, and re-layouts: 3.94 us -> 5.18 us
where the time goes in v5:
time: 120 us; the launch traced here: 119 us
  Pallas kernels  113 us (94%)
  local copies, waits for them, and re-layouts  5.18 us (4%)
    pallas_call x1, Pallas kernels, local(): pl.pallas_call(functools.partial(kernel, D, Q), out_shape=(jax.ShapeDtype...  113 us
    unnamed x3, local copies, waits for them, and re-layouts  5.18 us

profile of v5, /device:TPU:0, one launch (start us, length us, event | category | flops | bytes accessed | tf_op | source)
XLA Modules:
  0.0 118.8 jit_solution(6359626350866831395)
XLA Ops:
  0.6 113.0 %shard_map.67 = (f32[1,512]{1,0:T(1,128)}, bf16[512,256]{1,0:T(8,128)(2,1)}, bf16[2048,256]{1,0:T(8,128)(2,1)}) custom-call(bf16[512,256]{1,0:T(8,128)(2,1)} %tf.1, bf16[512,256]{1,0:T(8,128)(2,1)} %sf.1, bf16[16384,256]{1,0:T(8,128)(2,1)} %tp.1, bf16[16384,256]{1,0:T(8,128)(2,1)} %sp.1), custom_call_target="tpu_custom_call" | custom-call | tf_op jit(solution)/shard_map/pallas_call | solution.py:529
  113.7 1.3 %copy.10 = f32[512]{0:T(512)} copy(f32[512]{0:T(512)} %bitcast.1) | data formatting | bytes 4096
  114.9 1.7 %copy.11 = bf16[512,256]{1,0:T(8,128)(2,1)} copy(bf16[512,256]{1,0:T(8,128)(2,1)} %get-tuple-element.13) | data formatting | bytes 524288
  116.6 2.3 %copy.12 = bf16[2048,256]{1,0:T(8,128)(2,1)} copy(bf16[2048,256]{1,0:T(8,128)(2,1)} %get-tuple-element.14) | data formatting | bytes 2097152
